TPU v7x, 256 devices: a whole 4x4x8 slice. The times are simulated.
256 devices in a mesh: facet: 128 (over y, x, z), row: 2 (over core).
Axes of the slice: x: 4, y: 4, z: 8, core: 2. Of those that a mesh axis runs over, the one named last changes fastest.
Arguments:
- facet: bfloat16 [128, 2, 1024, 1024], P('facet', None, 'row'), may hold values from -6 to 6
- taper: float32 [1024], replicated, may hold values from 0.25 to 1
- shifts: int32 [128, 2, 4], P('facet'), may hold values from 0 to 1023
- cover: int32 [128, 4], P('facet'), may hold values 0 or 1
- phase: int32 [128, 4], P('facet'), may hold values from 0 to 1023
- owner: int32 [128], replicated, may hold values from 0 to 127, each once
Outputs:
- owned: float32 [128, 8, 512], P('facet', 'row')
Inputs may be any that keep to these rules, and one draw needn't show every extreme that they name: owner is a permutation: every owner slot receives exactly one strip.
All inputs are finite; a program needn't handle non-finite values. No bound on the sum of `cover` on one device may be relied on, other than what follows from the above.
Results may differ from a plain program's by a relative error of at most 0.0075.
Values may be sent and summed in bfloat16 or wider, within the bound.
No kernel may reach another device: no remote copies, remote signals or barrier semaphores. Data moves between devices by JAX's collectives and lax.ppermute only.
A program may use at most 64 MiB of HBM per device.

v0:
```python
import math

import jax
import jax.numpy as jnp
from jax import lax
from jax.sharding import PartitionSpec as P

F = 1024
SG = 256


def tables(shift, columns, taper_part):
    freqs = jnp.arange(SG, dtype=jnp.int32)
    index = (shift + freqs)[:, None] * columns[None, :] % F
    angles = index.astype(jnp.float32) * (2.0 * math.pi / F)
    weights = taper_part[None, :] / math.sqrt(F)
    return jnp.stack([jnp.cos(angles) * weights, -jnp.sin(angles) * weights], axis=0).astype(
        jnp.bfloat16
    )


def mixer_of(v_tab):
    top = jnp.concatenate([v_tab[0], -v_tab[1]], axis=1)
    bottom = jnp.concatenate([v_tab[1], v_tab[0]], axis=1)
    return jnp.concatenate([top, bottom], axis=0)


def first_pass(u_tab, facet_rows):
    products = jnp.einsum("ajx,bxy->abjy", u_tab, facet_rows, preferred_element_type=jnp.float32)
    real = products[0, 0] - products[1, 1]
    imag = products[0, 1] + products[1, 0]
    return jnp.concatenate([real, imag], axis=1).astype(jnp.bfloat16)


def rotate(image, cover_value, phase_value):
    angle = phase_value.astype(jnp.float32) * (2.0 * math.pi / F)
    cos_w = cover_value.astype(jnp.float32) * jnp.cos(angle)
    sin_w = cover_value.astype(jnp.float32) * jnp.sin(angle)
    real = image[:, :SG]
    imag = image[:, SG:]
    return jnp.concatenate([cos_w * real - sin_w * imag, sin_w * real + cos_w * imag], axis=1)


def per_device(facet, taper, shifts, cover, phase, owner):
    row_count = lax.axis_size("row")
    facet_count = lax.axis_size("facet")
    part_rows = facet.shape[2]
    row_start = lax.axis_index("row") * part_rows
    sub_count = shifts.shape[2]
    half_rows = SG // row_count
    strip_rows = sub_count * SG // (row_count * facet_count)
    columns = row_start + jnp.arange(part_rows, dtype=jnp.int32)
    taper_part = lax.dynamic_slice_in_dim(taper, row_start, part_rows)
    all_columns = jnp.arange(F, dtype=jnp.int32)
    positions = jnp.arange(owner.shape[0], dtype=jnp.int32)
    inverse = jnp.zeros_like(owner).at[owner].set(positions)
    partials = []
    for subgrid in range(sub_count):
        u_tab = tables(shifts[0, 0, subgrid], columns, taper_part)
        partials.append(first_pass(u_tab, facet[0]))
    stacked = jnp.stack(partials)
    swapped = lax.all_to_all(stacked, "row", split_axis=1, concat_axis=1, tiled=True)
    images = []
    for subgrid in range(sub_count):
        mixer = mixer_of(tables(shifts[0, 1, subgrid], all_columns, taper))
        grouped = swapped[subgrid].reshape(row_count, half_rows, 2 * F)
        image = jnp.einsum("ihy,ky->hk", grouped, mixer, preferred_element_type=jnp.float32)
        images.append(rotate(image, cover[0, subgrid], phase[0, subgrid]))
    strips = jnp.stack(images).reshape(facet_count, strip_rows, 2 * SG)
    summed = lax.psum_scatter(strips[inverse], "facet", scatter_dimension=0, tiled=True)
    return summed


def solution(mesh):
    return jax.shard_map(
        per_device,
        mesh=mesh,
        in_specs=(
            P("facet", None, "row", None),
            P(),
            P("facet", None, None),
            P("facet", None),
            P("facet", None),
            P(),
        ),
        out_specs=P("facet", "row", None),
        check_vma=False,
    )
```

profile of v0, /device:TPU:2, one launch (start us, length us, event | category | flops | bytes accessed | tf_op | source)
XLA Modules:
  0.0 358.0 jit_solution(3486545082899646957)
XLA Ops:
  6.5 1.7 fusion.118
  8.2 1.3 iota_add_fusion.5
  9.5 1.2 iota_add_fusion.7
  11.5 8.9 %multiply_convert_fusion.15 = (bf16[1,256,512]{2,1,0:T(8,128)(2,1)S(1)}, bf16[1,256,512]{2,1,0:T(8,128)(2,1)S(1)}, bf16[1,256,512]{2,1,0:T(8,128)(2,1)S(1)}, bf1...) fusion(f32[512]{0:T(512)S(1)} %dynamic-slice_multiply_fusion, ...), kind=kLoop, calls=%fused_computation.175 | loop fusion | flops 9961472 | bytes 2105344 | tf_op jit(solution)/shard_map/convert.34
  20.5 1.3 convolution_bitcast_fusion.3
  22.1 1.3 convolution_bitcast_fusion.2
  23.6 1.3 convolution_bitcast_fusion.1
  25.2 1.3 convolution_bitcast_fusion
  27.2 5.2 %copy.7 = bf16[4,256,2048]{2,0,1:T(4,128)(2,1)} copy(bf16[4,256,2048]{2,1,0:T(8,128)(2,1)S(1)} %maximum_maximum_fusion) | data formatting | bytes 8388608 | tf_op jit(solution)/shard_map/stack | solution.py:61
  32.5 5.7 %all-to-all-start = ((bf16[4,256,2048]{2,0,1:T(4,128)(2,1)}), bf16[4,256,2048]{2,0,1:T(4,128)(2,1)}, u32[]{:S(2)}, u32[]{:S(2)}) async-start(bf16[4,256,2048]{2,0,1:T(4,128)(2,1)} %copy.7), calls=%async_computation | async-start | bytes 8388608 | tf_op jit(solution)/shard_map/all_to_all | solution.py:62
  38.5 1.3 iota_add_fusion.1
  39.8 1.2 iota_add_fusion.3
  41.0 18.9 %fusion.81 = (bf16[256,1024]{1,0:T(8,128)(2,1)}, bf16[256,1024]{1,0:T(8,128)(2,1)}, bf16[256,1024]{1,0:T(8,128)(2,1)}, bf16[256,1024]{1,0:T(8,128)(2,1)}, bf16[2...) fusion(f32[1024]{0:T(1024)S(1)} %broadcast_multiply_fusion, ...), kind=kLoop, calls=%fused_computation.141 | loop fusion | flops 19922944 | bytes 4202496 | tf_op jit(solution)/shard_map/squeeze | solution.py:23
  59.9 17.2 %fusion.107 = (bf16[256,1024]{1,0:T(8,128)(2,1)}, bf16[256,1024]{1,0:T(8,128)(2,1)}, bf16[256,1024]{1,0:T(8,128)(2,1)S(1)}, bf16[256,1024]{1,0:T(8,128)(2,1)S(1)}) fusion(f32[1024]{0:T(1024)S(1)} %broadcast_multiply_fusion, s32[256]{0:T(256)S(1)} %get-tuple-element.80, s32[256]{0:T(256)S(1)} %get-tuple-element.79, s32[256]{0:T(256)S(1)} %get-tuple-element.78, ...), kind=kLoop, calls=%fused_computation.191 | loop fusion | flops 20971520 | bytes 2105344 | tf_op jit(solution)/shard_map/neg | solution.py:23
  80.9 14.6 %slice_convert_fusion.3 = (f32[1,256,2048]{2,0,1:T(1,128)S(1)}, f32[1,256,2048]{2,0,1:T(1,128)}, f32[1,256,2048]{2,0,1:T(1,128)}, f32[1,256,2048]{2,0,1:T(1,128)S(1)}) fusion(bf16[4,256,2048]{2,0,1:T(4,128)(2,1)} %all-to-all-done), kind=kLoop, calls=%fused_computation.10 | loop fusion | flops 2097152 | bytes 12582912 | tf_op jit(solution)/shard_map/ihy,ky->hk/convert_element_type | solution.py:67
  97.8 2.2 copy.13
  101.1 2.7 reduce_sum.37
  104.4 2.5 copy.14
  108.6 2.5 copy.15
  112.9 2.6 fusion
  120.4 1.5 reshape.1565
  122.9 2.1 gather_fusion
  125.7 223.5 %all-reduce.3.cloned.1.call-done = f32[128,4,512]{2,1,0:T(4,128)} async-done(((f32[128,4,512]{2,1,0:T(4,128)}), f32[128,4,512]{2,1,0:T(4,128)}) %all-reduce.3.cloned.1.call-update) | async-done | bytes 1048592
  349.2 2.0 constant_dynamic-slice_fusion
  (69 shorter events, 14.5 us)
Async XLA Ops:
  6.5 13.9 %copy-start = (bf16[1,2,512,1024]{3,2,1,0:T(8,128)(2,1)S(1)}, bf16[1,2,512,1024]{3,2,1,0:T(8,128)(2,1)}, u32[]{:S(2)}) copy-start(bf16[1,2,512,1024]{3,2,1,0:T(8,128)(2,1)} %param.6) | copy-start | bytes 6291460
  32.5 6.0 %copy-start.12 = (f32[1024]{0:T(1024)S(1)}, f32[1024]{0:T(1024)}, u32[]{:S(2)}) copy-start(f32[1024]{0:T(1024)} %param.7) | copy-start | bytes 12292
  32.5 48.4 %all-to-all-start = ((bf16[4,256,2048]{2,0,1:T(4,128)(2,1)}), bf16[4,256,2048]{2,0,1:T(4,128)(2,1)}, u32[]{:S(2)}, u32[]{:S(2)}) async-start(bf16[4,256,2048]{2,0,1:T(4,128)(2,1)} %copy.7), calls=%async_computation | async-start | bytes 8388608 | tf_op jit(solution)/shard_map/all_to_all | solution.py:62
  38.2 38.9 %copy-start.13 = (s32[1,4]{1,0:T(1,128)S(1)}, s32[1,4]{1,0:T(1,128)}, u32[]{:S(2)}) copy-start(s32[1,4]{1,0:T(1,128)} %param.10) | copy-start | bytes 52
  38.2 311.0 %all-reduce.3.cloned.1.call-start = ((), (), s32[]{:S(2)}) async-start(), calls=%async_computation.1 | async-start | bytes 2097152
  95.5 0.9 copy-start.14
  112.8 2.8 copy-start.2
  112.9 2.8 copy-start.5
  112.9 2.8 copy-start.10
  112.9 2.8 copy-start.11
  115.6 1.0 copy-start.4
  115.7 1.2 copy-start.8
  115.7 1.3 copy-start.9
  117.0 1.0 copy-start.3
  117.0 1.2 copy-start.6
  117.0 1.4 copy-start.7
  119.2 2.7 copy-start.15
  119.2 232.0 %copy-start.1 = (bf16[1,2,512,1024]{3,2,1,0:T(8,128)(2,1)S(1)}, bf16[1,2,512,1024]{3,2,1,0:T(8,128)(2,1)}, u32[]{:S(2)}) copy-start(bf16[1,2,512,1024]{3,2,1,0:T(8,128)(2,1)} %param.6) | copy-start | bytes 6291460
  119.2 5.8 %copy-start.16 = (u32[256]{0:T(256)S(1)}, u32[256]{0:T(256)}, u32[]{:S(2)}) copy-start(u32[256]{0:T(256)} %constant.85) | copy-start | bytes 3076
Sparse Core Ops, SparseCore 0:
  125.2 223.9 all-reduce.2
where the time goes:
time: 359 us; the launch traced here: 358 us
  waiting for transfers between devices  223 us (62%)
  other arithmetic  74.4 us (21%)
  local copies, waits for them, and re-layouts  24.4 us (7%)
  between operations  19.6 us (5%)
  matrix products  10.2 us (3%)
  starting transfers between devices  5.96 us (2%)
    unnamed x2, waiting for transfers between devices  223 us
    squeeze x1, other arithmetic, mixer_of(): top = jnp.concatenate([v_tab[0], -v_tab[1]], axis=1)  18.9 us
    neg x1, other arithmetic, mixer_of(): top = jnp.concatenate([v_tab[0], -v_tab[1]], axis=1)  17.2 us
    convert_element_type x1, other arithmetic, per_device(): jnp.einsum('ihy,ky->hk', grouped, mixer, preferred_element_type=jnp.float32)  14.6 us
    unnamed x40, local copies, waits for them, and re-layouts  11.6 us
    another operation x1, other arithmetic  8.9 us
  transfers between devices with their start and end apart: 2, of which 1 were waited for; matrix products, arithmetic and copies ran while one was open for 11% of the time, Pallas kernels for 0%

commit v1 on v0

v1 whole, which is shorter than its diff:
```python
import math

import jax
import jax.numpy as jnp
from jax import lax
from jax.experimental import pallas as pl
from jax.experimental.pallas import tpu as pltpu
from jax.sharding import PartitionSpec as P

F = 1024
SG = 256
NSUB = 4
RADIX = 4
Q = F // RADIX
J = SG // RADIX
HALF = J // 2
STRIPS = NSUB * HALF
ROWS = 16
LANES = 128
STEP = 2.0 * math.pi / F
BF = jnp.bfloat16
F32 = jnp.float32


def unit(index):
    angle = (index & (F - 1)).astype(F32) * STEP
    return jnp.cos(angle), -jnp.sin(angle)


def iota(shape, axis):
    return lax.broadcasted_iota(jnp.int32, shape, axis)


def by_subgrid(values, shape):
    group = iota(shape, 0) // RADIX
    out = jnp.full(shape, values[0])
    for s in range(1, NSUB):
        out = jnp.where(group == s, values[s], out)
    return out


def images(shifts, cover, phase, owner, half, taper, facet_hbm, keep, send,
           facet, grid, left, right, part, strips, columns, sem):
    copies = [
        pltpu.make_async_copy(facet_hbm.at[0, part_at], facet.at[part_at], sem.at[part_at])
        for part_at in range(2)
    ]
    for copy in copies:
        copy.start()
    h = half[0]

    low_r, low_i = unit(4 * iota((8, Q), 0) * iota((8, Q), 1))
    high_r, high_i = unit(32 * iota((8, Q), 0) * iota((8, Q), 1))
    comb_r = jnp.concatenate([low_r * high_r[u:u + 1] - low_i * high_i[u:u + 1] for u in range(J // 8)])
    comb_i = jnp.concatenate([low_r * high_i[u:u + 1] + low_i * high_r[u:u + 1] for u in range(J // 8)])
    shape = (NSUB * RADIX, Q)
    scale = 1.0 / math.sqrt(F)

    def write(table, at, row, rr, ri):
        re = comb_r * rr - comb_i * ri
        im = comb_r * ri + comb_i * rr
        re_b, im_b = re.astype(BF), im.astype(BF)
        table[at, row:row + J, :Q] = re_b
        table[at, row:row + J, Q:] = (-im).astype(BF)
        table[at, row + J:row + 2 * J, :Q] = im_b
        table[at, row + J:row + 2 * J, Q:] = re_b

    freq = by_subgrid([shifts[0, 0, s] for s in range(NSUB)], shape) + iota(shape, 0) % RADIX
    turn = by_subgrid([phase[0, s] for s in range(NSUB)], shape)
    gain = by_subgrid([cover[0, s].astype(F32) * scale for s in range(NSUB)], shape)
    row_r, row_i = unit(freq * (iota(shape, 1) + h * (F // 2)) - turn)
    row_r, row_i = row_r * gain, row_i * gain
    for s in range(NSUB):
        for t in range(RADIX):
            n = s * RADIX + t
            write(left, (shifts[0, 0, s] + t) & 3, s * 2 * J, row_r[n:n + 1], row_i[n:n + 1])
    freq = by_subgrid([shifts[0, 1, s] for s in range(NSUB)], shape) + iota(shape, 0) % RADIX
    row_r, row_i = unit(freq * iota(shape, 1))
    row_r, row_i = row_r * scale, row_i * scale
    for n in range(NSUB * RADIX):
        write(right, n, 0, row_r[n:n + 1], row_i[n:n + 1])

    for q in range(F // 2 // LANES):
        row = taper[pl.ds(h * 4 + q, 1), :]
        columns[q * LANES:(q + 1) * LANES, :] = jnp.transpose(jnp.broadcast_to(row, (LANES, LANES)))

    for copy in copies:
        copy.wait()

    rows = 16
    for v in range(Q // LANES):
        across = [jnp.broadcast_to(taper[2 * a + v:2 * a + v + 1, :], (rows, LANES)) for a in range(RADIX)]

        def block(i, carry):
            b = pl.multiple_of(i * rows, rows)
            lines = []
            for a in range(2):
                down = columns[pl.ds(a * Q + b, rows), :]
                z = []
                for c in range(RADIX):
                    weight = down * across[c]
                    lane = c * Q + v * LANES
                    z.append([
                        facet[p, pl.ds(a * Q + b, rows), lane:lane + LANES].astype(F32) * weight
                        for p in range(2)
                    ])
                e0 = [z[0][p] + z[2][p] for p in range(2)]
                e1 = [z[0][p] - z[2][p] for p in range(2)]
                o0 = [z[1][p] + z[3][p] for p in range(2)]
                o1 = [z[1][p] - z[3][p] for p in range(2)]
                lines.append([
                    (e0[0] + o0[0], e0[1] + o0[1]),
                    (e1[0] + o1[1], e1[1] - o1[0]),
                    (e0[0] - o0[0], e0[1] - o0[1]),
                    (e1[0] - o1[1], e1[1] + o1[0]),
                ])
            for c in range(RADIX):
                (ar, ai), (br, bi) = lines[0][c], lines[1][c]
                lane = c * Q + v * LANES
                outs = [(ar + br, ai + bi), (ar + bi, ai - br), (ar - br, ai - bi), (ar - bi, ai + br)]
                for x, pair in enumerate(outs):
                    for p in range(2):
                        grid[x, pl.ds(p * Q + b, rows), lane:lane + LANES] = pair[p].astype(BF)
            return carry

        lax.fori_loop(0, Q // rows, block, 0)

    for c in range(RADIX):
        slots = [(c - shifts[0, 0, s]) & 3 for s in range(NSUB)]
        for y in range(RADIX):
            sums = jnp.dot(left[c], grid[c, :, y * Q:(y + 1) * Q], preferred_element_type=F32).astype(BF)
            for s in range(NSUB):
                for p in range(2):
                    row = (2 * s + p) * J
                    part[s, slots[s], :, (2 * y + p) * Q:(2 * y + p + 1) * Q] = sums[row:row + J]

    for s in range(NSUB):
        for k in range(RADIX):
            lane = pl.multiple_of(((shifts[0, 1, s] + k) & 3) * (2 * Q), 2 * Q)
            rows_in = part[s, :, :, pl.ds(lane, 2 * Q)].reshape(SG, 2 * Q)
            image = lax.dot_general(rows_in, right[s * RADIX + k], (((1,), (1,)), ((), ())),
                                    preferred_element_type=F32)
            for t in range(RADIX):
                for r in range(2):
                    start = (r * NSUB + s) * HALF * ROWS + k * RADIX + t
                    row = t * J + r * HALF
                    strips[pl.ds(start, HALF, stride=ROWS), :] = image[row:row + HALF]

    def place(k, carry):
        to = owner[k]
        mine = pl.multiple_of((h * STRIPS + k) * ROWS, ROWS)
        theirs = pl.multiple_of(((1 - h) * STRIPS + k) * ROWS, ROWS)
        keep[to] = strips[pl.ds(mine, ROWS), :]
        send[to] = strips[pl.ds(theirs, ROWS), :].astype(BF)
        return carry

    lax.fori_loop(0, STRIPS, place, 0, unroll=8)


def total(parts, out):
    sums = parts[0].astype(F32)
    for i in range(1, parts.shape[0]):
        sums = sums + parts[i].astype(F32)
    lane, col = iota((LANES, 2 * SG), 0), iota((LANES, 2 * SG), 1)
    spread = (col == (lane // J) * SG + (lane % J) * RADIX).astype(F32)
    wide = jnp.dot(sums, spread, precision=lax.Precision.HIGHEST, preferred_element_type=F32)
    result = wide[:RADIX]
    for k in range(1, RADIX):
        result = result + pltpu.roll(wide[k * RADIX:(k + 1) * RADIX], k, 1)
    out[0] = result


def per_device(facet, taper, shifts, cover, phase, owner):
    smem = pl.BlockSpec(memory_space=pltpu.SMEM)
    vmem = pl.BlockSpec(memory_space=pltpu.VMEM)
    half = lax.axis_index("row").reshape(1)
    keep, send = pl.pallas_call(
        images,
        out_shape=(
            jax.ShapeDtypeStruct((STRIPS, ROWS, LANES), F32),
            jax.ShapeDtypeStruct((STRIPS, ROWS, LANES), BF),
        ),
        in_specs=[smem] * 5 + [vmem, pl.BlockSpec(memory_space=pl.ANY)],
        out_specs=(vmem, vmem),
        scratch_shapes=[
            pltpu.VMEM((2, F // 2, F), BF),
            pltpu.VMEM((RADIX, 2 * Q, F), BF),
            pltpu.VMEM((RADIX, NSUB * 2 * J, 2 * Q), BF),
            pltpu.VMEM((NSUB * RADIX, 2 * J, 2 * Q), BF),
            pltpu.VMEM((NSUB, RADIX, J, 2 * F), BF),
            pltpu.VMEM((2 * STRIPS * ROWS, LANES), F32),
            pltpu.VMEM((F // 2, LANES), F32),
            pltpu.SemaphoreType.DMA((2,)),
        ],
        compiler_params=pltpu.CompilerParams(vmem_limit_bytes=40 * 2**20),
        name="images",
    )(shifts, cover, phase, owner, half, taper.reshape(8, LANES), facet)
    with jax.named_scope("row_swap"):
        other = lax.ppermute(send, "row", [(0, 1), (1, 0)])
        merged = (keep + other.astype(F32)).astype(BF)
    with jax.named_scope("to_owners"):
        parts = lax.all_to_all(merged, "facet", split_axis=0, concat_axis=0, tiled=True)
    return pl.pallas_call(
        total,
        out_shape=jax.ShapeDtypeStruct((1, RADIX, 2 * SG), F32),
        in_specs=[vmem],
        out_specs=vmem,
        name="total",
    )(parts)


def solution(mesh):
    return jax.shard_map(
        per_device,
        mesh=mesh,
        in_specs=(
            P("facet", None, "row", None),
            P(),
            P("facet", None, None),
            P("facet", None),
            P("facet", None),
            P(),
        ),
        out_specs=P("facet", "row", None),
        check_vma=False,
    )
```

time: 359 us -> 52.5 us (0.15)
  the two profiles are of different devices: /device:TPU:2 before, /device:TPU:1 now
where the time goes in v1:
time: 52.5 us; the launch traced here: 52.2 us
  blocking collectives  33 us (63%)
  Pallas kernels  9.28 us (18%)
  local copies, waits for them, and re-layouts  4.92 us (9%)
  starting transfers between devices  3.33 us (6%)
  waiting for transfers between devices  1.54 us (3%)
    all_to_all x1, blocking collectives, per_device(): lax.all_to_all(merged, 'facet', split_axis=0, concat_axis=0, tiled=True)  33 us
    pallas_call x1, Pallas kernels, per_device(): pl.pallas_call(images, out_shape=(jax.ShapeDtypeStruct((STRIPS, ROWS, LAN...  7.16 us
    unnamed x12, local copies, waits for them, and re-layouts  4.92 us
    ppermute x1, starting transfers between devices, per_device(): other = lax.ppermute(send, 'row', [(0, 1), (1, 0)])  3.33 us
    pallas_call x1, Pallas kernels, per_device(): pl.pallas_call(total, out_shape=jax.ShapeDtypeStruct((1, RADIX, 2 * SG),...  2.13 us
    ppermute x1, waiting for transfers between devices, per_device(): other = lax.ppermute(send, 'row', [(0, 1), (1, 0)])  1.54 us
  transfers between devices with their start and end apart: 1, of which 1 were waited for; matrix products, arithmetic and copies ran while one was open for 0% of the time, Pallas kernels for 0%

profile of v1, /device:TPU:1, one launch (start us, length us, event | category | flops | bytes accessed | tf_op | source)
XLA Modules:
  0.0 52.2 jit_solution(4305170850590286019)
XLA Ops:
  0.0 0.0 copy-start
  0.0 1.6 %copy-done = bf16[1,2,512,1024]{3,2,1,0:T(8,128)(2,1)S(1)} copy-done((bf16[1,2,512,1024]{3,2,1,0:T(8,128)(2,1)S(1)}, bf16[1,2,512,1024]{3,2,1,0:T(8,128)(2,1)}, u32[]{:S(2)}) %copy-start) | copy-done | bytes 2097176
  1.6 0.0 copy-start.1
  1.6 0.7 %copy-done.1 = f32[1024]{0:T(1024)S(1)} copy-done((f32[1024]{0:T(1024)S(1)}, f32[1024]{0:T(1024)}, u32[]{:S(2)}) %copy-start.1) | copy-done | bytes 4120
  2.3 0.0 copy-start.2
  2.3 0.7 %copy-done.2 = s32[1,2,4]{2,1,0:T(2,128)S(1)} copy-done((s32[1,2,4]{2,1,0:T(2,128)S(1)}, s32[1,2,4]{2,1,0:T(2,128)}, u32[]{:S(2)}) %copy-start.2) | copy-done | bytes 56
  3.0 0.0 copy-start.3
  3.0 0.7 %copy-done.3 = s32[1,4]{1,0:T(1,128)S(1)} copy-done((s32[1,4]{1,0:T(1,128)S(1)}, s32[1,4]{1,0:T(1,128)}, u32[]{:S(2)}) %copy-start.3) | copy-done | bytes 40
  3.6 0.0 copy-start.4
  3.6 0.7 %copy-done.4 = s32[1,4]{1,0:T(1,128)S(1)} copy-done((s32[1,4]{1,0:T(1,128)S(1)}, s32[1,4]{1,0:T(1,128)}, u32[]{:S(2)}) %copy-start.4) | copy-done | bytes 40
  4.3 0.0 copy-start.5
  4.3 0.7 %copy-done.5 = s32[128]{0:T(128)S(1)} copy-done((s32[128]{0:T(128)S(1)}, s32[128]{0:T(128)}, u32[]{:S(2)}) %copy-start.5) | copy-done | bytes 536
  4.9 7.2 %images.1 = (f32[128,16,128]{2,1,0:T(8,128)S(1)}, bf16[128,16,128]{2,1,0:T(8,128)(2,1)S(1)}) custom-call(s32[1,2,4]{2,1,0:T(2,128)S(1)} %copy-done.2, s32[1,4]{1,0:T(1,128)S(1)} %copy-done.3, s32[1,4]{1,0:T(1,128)S(1)} %copy-done.4, s32[128]{0:T(128)S(1)} %copy-done.5, s32[1]{0:T(128)} %bitcast.half, f32[8,128]{1,0:T(8,128)S(1)} %bitcast.2, ...), custom_call_target="tpu_custom_call" | custom-call | tf_op jit(solution)/shard_map/images/pallas_call | solution.py:177
  12.1 3.3 %collective-permute-start = (bf16[128,16,128]{2,1,0:T(8,128)(2,1)S(1)}, bf16[128,16,128]{2,1,0:T(8,128)(2,1)S(1)}, u32[]{:S(2)}, u32[]{:S(2)}) collective-permute-start(bf16[128,16,128]{2,1,0:T(8,128)(2,1)S(1)} %get-tuple-element.8), channel_id=1, source_target_pairs={{0,1},{1,0},{2,3},{3,2},{4,5},{5,4},{6,7},{7,6},{8,9},{9,8},{10,11... | collective-permute-start | bytes 1572872 | tf_op jit(solution)/shard_map/row_swap/ppermute | solution.py:199
  15.4 1.5 %collective-permute-done = bf16[128,16,128]{2,1,0:T(8,128)(2,1)S(1)} collective-permute-done((bf16[128,16,128]{2,1,0:T(8,128)(2,1)S(1)}, bf16[128,16,128]{2,1,0:T(8,128)(2,1)S(1)}, u32[]{:S(2)}, u32[]{:S(2)}) %collective-permute-start) | collective-permute-done | bytes 524320 | tf_op jit(solution)/shard_map/row_swap/ppermute | solution.py:199
  17.0 0.1 add_convert_fusion
  17.1 33.0 %all_to_all.5.parts = bf16[128,16,128]{2,1,0:T(8,128)(2,1)} all-to-all(bf16[128,16,128]{2,1,0:T(8,128)(2,1)S(1)} %add_convert_fusion), channel_id=1, replica_groups=mesh['facet'=128,'row'=2] {'facet'}, dimensions={0} | all-to-all | bytes 1048576 | tf_op jit(solution)/shard_map/to_owners/all_to_all | solution.py:202
  50.1 2.1 %total.1 = f32[1,4,512]{2,1,0:T(4,128)} custom-call(bf16[128,16,128]{2,1,0:T(8,128)(2,1)} %all_to_all.5.parts), custom_call_target="tpu_custom_call" | custom-call | tf_op jit(solution)/shard_map/total/pallas_call | solution.py:203
Async XLA Ops:
  0.0 1.6 %copy-start = (bf16[1,2,512,1024]{3,2,1,0:T(8,128)(2,1)S(1)}, bf16[1,2,512,1024]{3,2,1,0:T(8,128)(2,1)}, u32[]{:S(2)}) copy-start(bf16[1,2,512,1024]{3,2,1,0:T(8,128)(2,1)} %facet_hbm.1) | copy-start | bytes 6291460
  1.6 0.7 %copy-start.1 = (f32[1024]{0:T(1024)S(1)}, f32[1024]{0:T(1024)}, u32[]{:S(2)}) copy-start(f32[1024]{0:T(1024)} %param.7) | copy-start | bytes 12292
  2.3 0.7 %copy-start.2 = (s32[1,2,4]{2,1,0:T(2,128)S(1)}, s32[1,2,4]{2,1,0:T(2,128)}, u32[]{:S(2)}) copy-start(s32[1,2,4]{2,1,0:T(2,128)} %shifts.1) | copy-start | bytes 100
  3.0 0.7 %copy-start.3 = (s32[1,4]{1,0:T(1,128)S(1)}, s32[1,4]{1,0:T(1,128)}, u32[]{:S(2)}) copy-start(s32[1,4]{1,0:T(1,128)} %cover.1) | copy-start | bytes 52
  3.6 0.7 %copy-start.4 = (s32[1,4]{1,0:T(1,128)S(1)}, s32[1,4]{1,0:T(1,128)}, u32[]{:S(2)}) copy-start(s32[1,4]{1,0:T(1,128)} %phase.1) | copy-start | bytes 52
  4.3 0.7 %copy-start.5 = (s32[128]{0:T(128)S(1)}, s32[128]{0:T(128)}, u32[]{:S(2)}) copy-start(s32[128]{0:T(128)} %owner.1) | copy-start | bytes 1540
  12.1 4.9 %collective-permute-start = (bf16[128,16,128]{2,1,0:T(8,128)(2,1)S(1)}, bf16[128,16,128]{2,1,0:T(8,128)(2,1)S(1)}, u32[]{:S(2)}, u32[]{:S(2)}) collective-permute-start(bf16[128,16,128]{2,1,0:T(8,128)(2,1)S(1)} %get-tuple-element.8), channel_id=1, source_target_pairs={{0,1},{1,0},{2,3},{3,2},{4,5},{5,4},{6,7},{7,6},{8,9},{9,8},{10,11... | collective-permute-start | bytes 1572872 | tf_op jit(solution)/shard_map/row_swap/ppermute | solution.py:199

commit v2 on v1

v2 whole, which is shorter than its diff:
```python
import math

import jax
import jax.numpy as jnp
from jax import lax
from jax.experimental import pallas as pl
from jax.experimental.pallas import tpu as pltpu
from jax.sharding import PartitionSpec as P

F = 1024
SG = 256
NSUB = 4
RADIX = 4
Q = F // RADIX
J = SG // RADIX
HALF = J // 2
STRIPS = NSUB * HALF
ROWS = 16
LANES = 128
STEP = 2.0 * math.pi / F
BF = jnp.bfloat16
F32 = jnp.float32


def unit(index):
    angle = (index & (F - 1)).astype(F32) * STEP
    return jnp.cos(angle), -jnp.sin(angle)


def iota(shape, axis):
    return lax.broadcasted_iota(jnp.int32, shape, axis)


def by_subgrid(values, shape):
    group = iota(shape, 0) // RADIX
    out = jnp.full(shape, values[0])
    for s in range(1, NSUB):
        out = jnp.where(group == s, values[s], out)
    return out


def images(shifts_in, cover_in, phase_in, owner_in, taper_in, facet_in, keep, send,
           shifts, cover, phase, owner, taper, facet, grid, left, right, part, strips, columns, sem):
    moves = [(shifts_in, shifts), (cover_in, cover), (phase_in, phase), (owner_in, owner), (taper_in, taper)]
    small = [pltpu.make_async_copy(src, dst, sem.at[n]) for n, (src, dst) in enumerate(moves)]
    copies = [
        pltpu.make_async_copy(facet_in.at[0, p], facet.at[p], sem.at[len(moves) + p]) for p in range(2)
    ]
    for copy in small + copies:
        copy.start()
    h = lax.axis_index("row")

    low_r, low_i = unit(4 * iota((8, Q), 0) * iota((8, Q), 1))
    high_r, high_i = unit(32 * iota((8, Q), 0) * iota((8, Q), 1))
    comb_r = jnp.concatenate([low_r * high_r[u:u + 1] - low_i * high_i[u:u + 1] for u in range(J // 8)])
    comb_i = jnp.concatenate([low_r * high_i[u:u + 1] + low_i * high_r[u:u + 1] for u in range(J // 8)])
    shape = (NSUB * RADIX, Q)
    scale = 1.0 / math.sqrt(F)

    def write(table, at, row, rr, ri):
        re = comb_r * rr - comb_i * ri
        im = comb_r * ri + comb_i * rr
        re_b, im_b = re.astype(BF), im.astype(BF)
        table[at, row:row + J, :Q] = re_b
        table[at, row:row + J, Q:] = (-im).astype(BF)
        table[at, row + J:row + 2 * J, :Q] = im_b
        table[at, row + J:row + 2 * J, Q:] = re_b

    for copy in small:
        copy.wait()
    freq = by_subgrid([shifts[0, 0, s] for s in range(NSUB)], shape) + iota(shape, 0) % RADIX
    turn = by_subgrid([phase[0, s] for s in range(NSUB)], shape)
    gain = by_subgrid([cover[0, s].astype(F32) * scale for s in range(NSUB)], shape)
    row_r, row_i = unit(freq * (iota(shape, 1) + h * (F // 2)) - turn)
    row_r, row_i = row_r * gain, row_i * gain
    for s in range(NSUB):
        for t in range(RADIX):
            n = s * RADIX + t
            write(left, (shifts[0, 0, s] + t) & 3, s * 2 * J, row_r[n:n + 1], row_i[n:n + 1])
    freq = by_subgrid([shifts[0, 1, s] for s in range(NSUB)], shape) + iota(shape, 0) % RADIX
    row_r, row_i = unit(freq * iota(shape, 1))
    row_r, row_i = row_r * scale, row_i * scale
    for n in range(NSUB * RADIX):
        at = n // RADIX * RADIX + ((shifts[0, 1, n // RADIX] + n) & 3)
        write(right, at, 0, row_r[n:n + 1], row_i[n:n + 1])

    for q in range(F // 2 // LANES):
        row = taper[pl.ds(h * 4 + q, 1), :]
        columns[q * LANES:(q + 1) * LANES, :] = jnp.transpose(jnp.broadcast_to(row, (LANES, LANES)))

    for copy in copies:
        copy.wait()

    def butterfly(b, v, across):
        lines = []
        for a in range(2):
            down = columns[pl.ds(a * Q + b, ROWS), :]
            z = []
            for c in range(RADIX):
                weight = down * across[c]
                lane = c * Q + v * LANES
                z.append([
                    facet[p, pl.ds(a * Q + b, ROWS), lane:lane + LANES].astype(F32) * weight
                    for p in range(2)
                ])
            e0 = [z[0][p] + z[2][p] for p in range(2)]
            e1 = [z[0][p] - z[2][p] for p in range(2)]
            o0 = [z[1][p] + z[3][p] for p in range(2)]
            o1 = [z[1][p] - z[3][p] for p in range(2)]
            lines.append([
                (e0[0] + o0[0], e0[1] + o0[1]),
                (e1[0] + o1[1], e1[1] - o1[0]),
                (e0[0] - o0[0], e0[1] - o0[1]),
                (e1[0] - o1[1], e1[1] + o1[0]),
            ])
        for c in range(RADIX):
            (ar, ai), (br, bi) = lines[0][c], lines[1][c]
            lane = (v * RADIX + c) * LANES
            outs = [(ar + br, ai + bi), (ar + bi, ai - br), (ar - br, ai - bi), (ar - bi, ai + br)]
            for x, pair in enumerate(outs):
                for p in range(2):
                    grid[x, pl.ds(p * Q + b, ROWS), lane:lane + LANES] = pair[p].astype(BF)

    def first(c, v, y):
        lane = (v * RADIX + y) * LANES
        sums = jnp.dot(left[c], grid[c, :, lane:lane + 2 * LANES], preferred_element_type=F32).astype(BF)
        for s in range(NSUB):
            for p in range(2):
                row = (2 * s + p) * J
                for i in range(2):
                    to = (2 * (y + i) + p) * Q + v * LANES
                    part[s, c, :, to:to + LANES] = sums[row:row + J, i * LANES:(i + 1) * LANES]

    def rim(v):
        return [jnp.broadcast_to(taper[2 * a + v:2 * a + v + 1, :], (ROWS, LANES)) for a in range(RADIX)]

    blocks = Q // ROWS
    edges = rim(0)

    def step(i, carry):
        butterfly(pl.multiple_of(i * ROWS, ROWS), 0, edges)
        return carry

    lax.fori_loop(0, blocks, step, 0, unroll=4)
    tiles = [(c, y) for c in range(RADIX) for y in (0, 2)]
    edges = rim(1)
    if True:
        for n, (c, y) in enumerate(tiles):
            for i in range(n * blocks // 8, (n + 1) * blocks // 8):
                butterfly(i * ROWS, 1, edges)
            first(c, 0, y)
    else:
        def step1(i, carry):
            butterfly(pl.multiple_of(i * ROWS, ROWS), 1, edges)
            return carry
        lax.fori_loop(0, blocks, step1, 0, unroll=4)
        for c, y in tiles:
            first(c, 0, y)
    for c, y in tiles:
        first(c, 1, y)

    for s in range(NSUB):
        for y in range(RADIX):
            k = (y - shifts[0, 1, s]) & 3
            rows_in = part[s, :, :, 2 * Q * y:2 * Q * (y + 1)].reshape(SG, 2 * Q)
            image = lax.dot_general(rows_in, right[s * RADIX + y], (((1,), (1,)), ((), ())),
                                    preferred_element_type=F32)
            for c in range(RADIX):
                t = (c - shifts[0, 0, s]) & 3
                for r in range(2):
                    start = r * HALF * ROWS + k * RADIX + t
                    row = c * J + r * HALF
                    strips[s, pl.ds(start, HALF, stride=ROWS), :] = image[row:row + HALF]
        for b in range(HALF):
            to = owner[s * HALF + b]
            mine = pl.multiple_of((h * HALF + b) * ROWS, ROWS)
            theirs = pl.multiple_of(((1 - h) * HALF + b) * ROWS, ROWS)
            keep[to] = strips[s, pl.ds(mine, ROWS), :]
            send[to] = strips[s, pl.ds(theirs, ROWS), :].astype(BF)


def total(parts_in, out, parts, sem):
    half = STRIPS // 2
    copies = [
        pltpu.make_async_copy(parts_in.at[pl.ds(i * half, half)], parts.at[pl.ds(i * half, half)], sem.at[i])
        for i in range(2)
    ]
    for copy in copies:
        copy.start()
    lane, col = iota((LANES, 2 * SG), 0), iota((LANES, 2 * SG), 1)
    spread = (col == (lane // J) * SG + (lane % J) * RADIX).astype(F32).astype(BF)
    sums = [jnp.zeros((ROWS, LANES), F32)] * 8
    for i in range(STRIPS):
        if i % half == 0:
            copies[i // half].wait()
        sums[i % 8] = sums[i % 8] + parts[i].astype(F32)
    while len(sums) > 1:
        sums = [a + b for a, b in zip(sums[::2], sums[1::2])]
    high = sums[0].astype(BF)
    rest = sums[0] - high.astype(F32)
    middle = rest.astype(BF)
    low = (rest - middle.astype(F32)).astype(BF)
    wide = jnp.dot(jnp.concatenate([high, middle, low]), spread, preferred_element_type=F32)
    wide = wide[:ROWS] + (wide[ROWS:2 * ROWS] + wide[2 * ROWS:])
    result = wide[:RADIX]
    for k in range(1, RADIX):
        result = result + pltpu.roll(wide[k * RADIX:(k + 1) * RADIX], k, 1)
    out[0] = result


def per_device(facet, taper, shifts, cover, phase, owner):
    anywhere = pl.BlockSpec(memory_space=pl.ANY)
    vmem = pl.BlockSpec(memory_space=pltpu.VMEM)
    strips = (STRIPS, ROWS, LANES)
    given = [
        pltpu.with_memory_space_constraint(x, pltpu.HBM)
        for x in (shifts, cover, phase, owner, taper.reshape(8, LANES), facet)
    ]
    keep, send = pl.pallas_call(
        images,
        out_shape=(jax.ShapeDtypeStruct(strips, F32), jax.ShapeDtypeStruct(strips, BF)),
        in_specs=[anywhere] * 6,
        out_specs=(vmem, vmem),
        scratch_shapes=[
            pltpu.SMEM(shifts.shape, jnp.int32),
            pltpu.SMEM(cover.shape, jnp.int32),
            pltpu.SMEM(phase.shape, jnp.int32),
            pltpu.SMEM(owner.shape, jnp.int32),
            pltpu.VMEM((8, LANES), F32),
            pltpu.VMEM((2, F // 2, F), BF),
            pltpu.VMEM((RADIX, 2 * Q, F), BF),
            pltpu.VMEM((RADIX, NSUB * 2 * J, 2 * Q), BF),
            pltpu.VMEM((NSUB * RADIX, 2 * J, 2 * Q), BF),
            pltpu.VMEM((NSUB, RADIX, J, 2 * F), BF),
            pltpu.VMEM((NSUB, SG // RADIX * ROWS, LANES), F32),
            pltpu.VMEM((F // 2, LANES), F32),
            pltpu.SemaphoreType.DMA((7,)),
        ],
        compiler_params=pltpu.CompilerParams(vmem_limit_bytes=40 * 2**20),
        name="images",
    )(*given)
    with jax.named_scope("row_swap"):
        other = lax.ppermute(send, "row", [(0, 1), (1, 0)])
        merged = (keep + other.astype(F32)).astype(BF)
    with jax.named_scope("to_owners"):
        parts = lax.all_to_all(merged, "facet", split_axis=0, concat_axis=0, tiled=True)
    return pl.pallas_call(
        total,
        out_shape=jax.ShapeDtypeStruct((1, RADIX, 2 * SG), F32),
        in_specs=[anywhere],
        out_specs=vmem,
        scratch_shapes=[pltpu.VMEM(strips, BF), pltpu.SemaphoreType.DMA((2,))],
        name="total",
    )(parts)


def solution(mesh):
    return jax.shard_map(
        per_device,
        mesh=mesh,
        in_specs=(
            P("facet", None, "row", None),
            P(),
            P("facet", None, None),
            P("facet", None),
            P("facet", None),
            P(),
        ),
        out_specs=P("facet", "row", None),
        check_vma=False,
    )
```

time: 52.5 us -> 47 us (0.90)
  local copies, waits for them, and re-layouts: 4.92 us -> 0 us
    unnamed x12 -> x0, local copies, waits for them, and re-layouts: 4.92 us -> none
where the time goes in v2:
time: 47 us; the launch traced here: 46.8 us
  blocking collectives  33 us (70%)
  Pallas kernels  8.87 us (19%)
  starting transfers between devices  3.33 us (7%)
  waiting for transfers between devices  1.54 us (3%)
    all_to_all x1, blocking collectives, per_device(): lax.all_to_all(merged, 'facet', split_axis=0, concat_axis=0, tiled=True)  33 us
    pallas_call x1, Pallas kernels, per_device(): pl.pallas_call(images, out_shape=(jax.ShapeDtypeStruct(strips, F32), jax....  6.97 us
    ppermute x1, starting transfers between devices, per_device(): other = lax.ppermute(send, 'row', [(0, 1), (1, 0)])  3.33 us
    pallas_call x1, Pallas kernels, per_device(): pl.pallas_call(total, out_shape=jax.ShapeDtypeStruct((1, RADIX, 2 * SG),...  1.9 us
    ppermute x1, waiting for transfers between devices, per_device(): other = lax.ppermute(send, 'row', [(0, 1), (1, 0)])  1.54 us
  transfers between devices with their start and end apart: 1, of which 1 were waited for; matrix products, arithmetic and copies ran while one was open for 0% of the time, Pallas kernels for 0%

profile of v2, /device:TPU:1, one launch (start us, length us, event | category | flops | bytes accessed | tf_op | source)
XLA Modules:
  0.0 46.8 jit_solution(2165523140724524171)
XLA Ops:
  0.0 7.0 %images.1 = (f32[128,16,128]{2,1,0:T(8,128)S(1)}, bf16[128,16,128]{2,1,0:T(8,128)(2,1)S(1)}) custom-call(s32[1,2,4]{2,1,0:T(2,128)} %shifts_in.1, s32[1,4]{1,0:T(1,128)} %cover_in.1, s32[1,4]{1,0:T(1,128)} %phase_in.1, s32[128]{0:T(128)} %owner_in.1, f32[8,128]{1,0:T(8,128)} %bitcast.1, bf16[1,2,512,1024]{3,2,1,0:T(8,128)(2,1)} %facet_in.1), custom_call_target="tpu_custom_call" | custom-call | tf_op jit(solution)/shard_map/images/pallas_call | solution.py:219
  7.0 3.3 %collective-permute-start = (bf16[128,16,128]{2,1,0:T(8,128)(2,1)S(1)}, bf16[128,16,128]{2,1,0:T(8,128)(2,1)S(1)}, u32[]{:S(2)}, u32[]{:S(2)}) collective-permute-start(bf16[128,16,128]{2,1,0:T(8,128)(2,1)S(1)} %get-tuple-element.8), channel_id=1, source_target_pairs={{0,1},{1,0},{2,3},{3,2},{4,5},{5,4},{6,7},{7,6},{8,9},{9,8},{10,11... | collective-permute-start | bytes 1572872 | tf_op jit(solution)/shard_map/row_swap/ppermute | solution.py:243
  10.3 1.5 %collective-permute-done = bf16[128,16,128]{2,1,0:T(8,128)(2,1)S(1)} collective-permute-done((bf16[128,16,128]{2,1,0:T(8,128)(2,1)S(1)}, bf16[128,16,128]{2,1,0:T(8,128)(2,1)S(1)}, u32[]{:S(2)}, u32[]{:S(2)}) %collective-permute-start) | collective-permute-done | bytes 524320 | tf_op jit(solution)/shard_map/row_swap/ppermute | solution.py:243
  11.8 0.1 add_convert_fusion
  12.0 33.0 %all_to_all.5.parts_in = bf16[128,16,128]{2,1,0:T(8,128)(2,1)} all-to-all(bf16[128,16,128]{2,1,0:T(8,128)(2,1)S(1)} %add_convert_fusion), channel_id=1, replica_groups=mesh['facet'=128,'row'=2] {'facet'}, dimensions={0} | all-to-all | bytes 1048576 | tf_op jit(solution)/shard_map/to_owners/all_to_all | solution.py:246
  44.9 1.9 %total.1 = f32[1,4,512]{2,1,0:T(4,128)} custom-call(bf16[128,16,128]{2,1,0:T(8,128)(2,1)} %all_to_all.5.parts_in), custom_call_target="tpu_custom_call" | custom-call | tf_op jit(solution)/shard_map/total/pallas_call | solution.py:247
Async XLA Ops:
  7.0 4.9 %collective-permute-start = (bf16[128,16,128]{2,1,0:T(8,128)(2,1)S(1)}, bf16[128,16,128]{2,1,0:T(8,128)(2,1)S(1)}, u32[]{:S(2)}, u32[]{:S(2)}) collective-permute-start(bf16[128,16,128]{2,1,0:T(8,128)(2,1)S(1)} %get-tuple-element.8), channel_id=1, source_target_pairs={{0,1},{1,0},{2,3},{3,2},{4,5},{5,4},{6,7},{7,6},{8,9},{9,8},{10,11... | collective-permute-start | bytes 1572872 | tf_op jit(solution)/shard_map/row_swap/ppermute | solution.py:243

commit v3 on v2

--- a/solution.py
+++ b/solution.py
@@ -5,7 +5,7 @@
 from jax import lax
 from jax.experimental import pallas as pl
 from jax.experimental.pallas import tpu as pltpu
-from jax.sharding import PartitionSpec as P
+from jax.sharding import Mesh, PartitionSpec as P
 
 F = 1024
 SG = 256
@@ -179,21 +179,19 @@
             send[to] = strips[s, pl.ds(theirs, ROWS), :].astype(BF)
 
 
-def total(parts_in, out, parts, sem):
-    half = STRIPS // 2
-    copies = [
-        pltpu.make_async_copy(parts_in.at[pl.ds(i * half, half)], parts.at[pl.ds(i * half, half)], sem.at[i])
-        for i in range(2)
-    ]
-    for copy in copies:
-        copy.start()
+def column(parts, out):
+    depth = out.shape[0]
+    for z in range(depth):
+        sums = [parts[i + z].astype(F32) for i in range(0, STRIPS, depth)]
+        while len(sums) > 1:
+            sums = [a + b for a, b in zip(sums[::2], sums[1::2])]
+        out[z] = sums[0].astype(BF)
+
+
+def total(parts, out):
     lane, col = iota((LANES, 2 * SG), 0), iota((LANES, 2 * SG), 1)
     spread = (col == (lane // J) * SG + (lane % J) * RADIX).astype(F32).astype(BF)
-    sums = [jnp.zeros((ROWS, LANES), F32)] * 8
-    for i in range(STRIPS):
-        if i % half == 0:
-            copies[i // half].wait()
-        sums[i % 8] = sums[i % 8] + parts[i].astype(F32)
+    sums = [parts[i].astype(F32) for i in range(parts.shape[0])]
     while len(sums) > 1:
         sums = [a + b for a, b in zip(sums[::2], sums[1::2])]
     high = sums[0].astype(BF)
@@ -242,30 +240,42 @@
     with jax.named_scope("row_swap"):
         other = lax.ppermute(send, "row", [(0, 1), (1, 0)])
         merged = (keep + other.astype(F32)).astype(BF)
+    with jax.named_scope("to_columns"):
+        parts = lax.all_to_all(merged, "plane", split_axis=0, concat_axis=0, tiled=True)
+    depth = lax.axis_size("line")
+    summed = pl.pallas_call(
+        column,
+        out_shape=jax.ShapeDtypeStruct((depth, ROWS, LANES), BF),
+        in_specs=[vmem],
+        out_specs=vmem,
+        name="column",
+    )(pltpu.with_memory_space_constraint(parts, pltpu.VMEM))
     with jax.named_scope("to_owners"):
-        parts = lax.all_to_all(merged, "facet", split_axis=0, concat_axis=0, tiled=True)
+        parts = lax.all_to_all(summed, "line", split_axis=0, concat_axis=0, tiled=True)
     return pl.pallas_call(
         total,
         out_shape=jax.ShapeDtypeStruct((1, RADIX, 2 * SG), F32),
-        in_specs=[anywhere],
+        in_specs=[vmem],
         out_specs=vmem,
-        scratch_shapes=[pltpu.VMEM(strips, BF), pltpu.SemaphoreType.DMA((2,))],
         name="total",
-    )(parts)
+    )(pltpu.with_memory_space_constraint(parts, pltpu.VMEM))
 
 
 def solution(mesh):
+    line = 8
+    grid = Mesh(mesh.devices.reshape(-1, line, mesh.devices.shape[1]), ("plane", "line", "row"))
+    facet = ("plane", "line")
     return jax.shard_map(
         per_device,
-        mesh=mesh,
+        mesh=grid,
         in_specs=(
-            P("facet", None, "row", None),
+            P(facet, None, "row", None),
             P(),
-            P("facet", None, None),
-            P("facet", None),
-            P("facet", None),
+            P(facet, None, None),
+            P(facet, None),
+            P(facet, None),
             P(),
         ),
-        out_specs=P("facet", "row", None),
+        out_specs=P(facet, "row", None),
         check_vma=False,
     )

time: 47 us -> 45 us (0.957)
  the two profiles are of different devices: /device:TPU:1 before, /device:TPU:2 now
where the time goes in v3:
time: 45 us; the launch traced here: 44.8 us
  blocking collectives  34.2 us (76%)
  Pallas kernels  8.5 us (19%)
  waiting for transfers between devices  1.9 us (4%)
    all_to_all x1, blocking collectives, per_device(): lax.all_to_all(merged, 'plane', split_axis=0, concat_axis=0, tiled=True)  17.7 us
    all_to_all x1, blocking collectives, per_device(): lax.all_to_all(summed, 'line', split_axis=0, concat_axis=0, tiled=True)  16.5 us
    pallas_call x1, Pallas kernels, per_device(): pl.pallas_call(images, out_shape=(jax.ShapeDtypeStruct(strips, F32), jax....  6.98 us
    ppermute x1, waiting for transfers between devices, per_device(): other = lax.ppermute(send, 'row', [(0, 1), (1, 0)])  1.9 us
  transfers between devices with their start and end apart: 1, of which 1 were waited for; matrix products, arithmetic and copies ran while one was open for 0% of the time, Pallas kernels for 0%

profile of v3, /device:TPU:2, one launch (start us, length us, event | category | flops | bytes accessed | tf_op | source)
XLA Modules:
  0.0 44.8 jit_solution(11283388035456424095)
XLA Ops:
  0.0 7.0 %images.1 = (f32[128,16,128]{2,1,0:T(8,128)S(1)}, bf16[128,16,128]{2,1,0:T(8,128)(2,1)S(1)}) custom-call(s32[1,2,4]{2,1,0:T(2,128)} %shifts_in.1, s32[1,4]{1,0:T(1,128)} %cover_in.1, s32[1,4]{1,0:T(1,128)} %phase_in.1, s32[128]{0:T(128)} %owner_in.1, f32[8,128]{1,0:T(8,128)} %bitcast.1, bf16[1,2,512,1024]{3,2,1,0:T(8,128)(2,1)} %facet_in.1), custom_call_target="tpu_custom_call" | custom-call | tf_op jit(solution)/shard_map/images/pallas_call | solution.py:217
  7.0 0.1 collective-permute-start
  7.1 1.9 %collective-permute-done = bf16[128,16,128]{2,1,0:T(8,128)(2,1)S(1)} collective-permute-done((bf16[128,16,128]{2,1,0:T(8,128)(2,1)S(1)}, bf16[128,16,128]{2,1,0:T(8,128)(2,1)S(1)}, u32[]{:S(2)}, u32[]{:S(2)}) %collective-permute-start) | collective-permute-done | bytes 524320 | tf_op jit(solution)/shard_map/row_swap/ppermute | solution.py:241
  9.0 0.1 add_convert_fusion
  9.1 17.7 %all_to_all.10.parts = bf16[128,16,128]{2,1,0:T(8,128)(2,1)S(1)} all-to-all(bf16[128,16,128]{2,1,0:T(8,128)(2,1)S(1)} %add_convert_fusion), channel_id=1, replica_groups=mesh['plane'=16,'line'=8,'row'=2] {'plane'}, dimensions={0} | all-to-all | bytes 1048576 | tf_op jit(solution)/shard_map/to_columns/all_to_all | solution.py:244
  26.8 0.7 %column.1 = bf16[8,16,128]{2,1,0:T(8,128)(2,1)} custom-call(bf16[128,16,128]{2,1,0:T(8,128)(2,1)S(1)} %all_to_all.10.parts), custom_call_target="tpu_custom_call" | custom-call | tf_op jit(solution)/shard_map/column/pallas_call | solution.py:246
  27.5 16.5 %all_to_all.11.parts = bf16[8,16,128]{2,1,0:T(8,128)(2,1)S(1)} all-to-all(bf16[8,16,128]{2,1,0:T(8,128)(2,1)} %column.1), channel_id=1, replica_groups=mesh['plane'=16,'line'=8,'row'=2] {'line'}, dimensions={0} | all-to-all | bytes 65536 | tf_op jit(solution)/shard_map/to_owners/all_to_all | solution.py:254
  44.0 0.8 %total.1 = f32[1,4,512]{2,1,0:T(4,128)} custom-call(bf16[8,16,128]{2,1,0:T(8,128)(2,1)S(1)} %all_to_all.11.parts), custom_call_target="tpu_custom_call" | custom-call | tf_op jit(solution)/shard_map/total/pallas_call | solution.py:255
Async XLA Ops:
  7.0 2.0 %collective-permute-start = (bf16[128,16,128]{2,1,0:T(8,128)(2,1)S(1)}, bf16[128,16,128]{2,1,0:T(8,128)(2,1)S(1)}, u32[]{:S(2)}, u32[]{:S(2)}) collective-permute-start(bf16[128,16,128]{2,1,0:T(8,128)(2,1)S(1)} %get-tuple-element.8), channel_id=1, source_target_pairs={{0,1},{1,0},{2,3},{3,2},{4,5},{5,4},{6,7},{7,6},{8,9},{9,8},{10,11... | collective-permute-start | bytes 1572872 | tf_op jit(solution)/shard_map/row_swap/ppermute | solution.py:241

commit v4 on v3

--- a/solution.py
+++ b/solution.py
@@ -18,6 +18,7 @@
 ROWS = 16
 LANES = 128
 STEP = 2.0 * math.pi / F
+CHUNKS = 4
 BF = jnp.bfloat16
 F32 = jnp.float32
 
@@ -39,13 +40,32 @@
     return out
 
 
-def images(shifts_in, cover_in, phase_in, owner_in, taper_in, facet_in, keep, send,
-           shifts, cover, phase, owner, taper, facet, grid, left, right, part, strips, columns, sem):
+def second(half, shifts, owner, right, part, strips, out):
+    for s in range(NSUB):
+        for y in range(RADIX):
+            k = (y - shifts[0, 1, s]) & 3
+            rows = pl.ds(pl.multiple_of(half * HALF, HALF), HALF)
+            rows_in = part[s, :, rows, 2 * Q * y:2 * Q * (y + 1)].reshape(SG // 2, 2 * Q)
+            image = lax.dot_general(rows_in, right[s * RADIX + y], (((1,), (1,)), ((), ())),
+                                    preferred_element_type=F32)
+            for c in range(RADIX):
+                t = (c - shifts[0, 0, s]) & 3
+                strips[s, pl.ds(k * RADIX + t, HALF, stride=ROWS), :] = image[c * HALF:(c + 1) * HALF]
+        for b in range(HALF):
+            out[owner[s * HALF + b]] = strips[s, b * ROWS:(b + 1) * ROWS, :].astype(out.dtype)
+
+
+def images(shifts_in, cover_in, phase_in, owner_in, taper_in, facet_in, send, part, right,
+           shifts, cover, phase, owner, taper, facet, grid, left, strips, columns, sem):
     moves = [(shifts_in, shifts), (cover_in, cover), (phase_in, phase), (owner_in, owner), (taper_in, taper)]
     small = [pltpu.make_async_copy(src, dst, sem.at[n]) for n, (src, dst) in enumerate(moves)]
-    copies = [
-        pltpu.make_async_copy(facet_in.at[0, p], facet.at[p], sem.at[len(moves) + p]) for p in range(2)
-    ]
+    copies = []
+    for g in range(CHUNKS):
+        for p in range(2):
+            for a in range(2):
+                rows = pl.ds(a * Q + g * Q // CHUNKS, Q // CHUNKS)
+                n = len(moves) + len(copies)
+                copies.append(pltpu.make_async_copy(facet_in.at[0, p, rows], facet.at[p, rows], sem.at[n]))
     for copy in small + copies:
         copy.start()
     h = lax.axis_index("row")
@@ -87,9 +107,6 @@
     for q in range(F // 2 // LANES):
         row = taper[pl.ds(h * 4 + q, 1), :]
         columns[q * LANES:(q + 1) * LANES, :] = jnp.transpose(jnp.broadcast_to(row, (LANES, LANES)))
-
-    for copy in copies:
-        copy.wait()
 
     def butterfly(b, v, across):
         lines = []
@@ -141,7 +158,10 @@
         butterfly(pl.multiple_of(i * ROWS, ROWS), 0, edges)
         return carry
 
-    lax.fori_loop(0, blocks, step, 0, unroll=4)
+    for g in range(CHUNKS):
+        for copy in copies[4 * g:4 * g + 4]:
+            copy.wait()
+        lax.fori_loop(g * blocks // CHUNKS, (g + 1) * blocks // CHUNKS, step, 0, unroll=4)
     tiles = [(c, y) for c in range(RADIX) for y in (0, 2)]
     edges = rim(1)
     if True:
@@ -159,24 +179,19 @@
     for c, y in tiles:
         first(c, 1, y)
 
-    for s in range(NSUB):
-        for y in range(RADIX):
-            k = (y - shifts[0, 1, s]) & 3
-            rows_in = part[s, :, :, 2 * Q * y:2 * Q * (y + 1)].reshape(SG, 2 * Q)
-            image = lax.dot_general(rows_in, right[s * RADIX + y], (((1,), (1,)), ((), ())),
-                                    preferred_element_type=F32)
-            for c in range(RADIX):
-                t = (c - shifts[0, 0, s]) & 3
-                for r in range(2):
-                    start = r * HALF * ROWS + k * RADIX + t
-                    row = c * J + r * HALF
-                    strips[s, pl.ds(start, HALF, stride=ROWS), :] = image[row:row + HALF]
-        for b in range(HALF):
-            to = owner[s * HALF + b]
-            mine = pl.multiple_of((h * HALF + b) * ROWS, ROWS)
-            theirs = pl.multiple_of(((1 - h) * HALF + b) * ROWS, ROWS)
-            keep[to] = strips[s, pl.ds(mine, ROWS), :]
-            send[to] = strips[s, pl.ds(theirs, ROWS), :].astype(BF)
+    second(1 - h, shifts, owner, right, part, strips, send)
+
+
+def kept(shifts_in, owner_in, right, part, keep, shifts, owner, strips, sem):
+    copies = [
+        pltpu.make_async_copy(src, dst, sem.at[n])
+        for n, (src, dst) in enumerate([(shifts_in, shifts), (owner_in, owner)])
+    ]
+    for copy in copies:
+        copy.start()
+    for copy in copies:
+        copy.wait()
+    second(lax.axis_index("row"), shifts, owner, right, part, strips, keep)
 
 
 def column(parts, out):
@@ -214,11 +229,16 @@
         pltpu.with_memory_space_constraint(x, pltpu.HBM)
         for x in (shifts, cover, phase, owner, taper.reshape(8, LANES), facet)
     ]
-    keep, send = pl.pallas_call(
+    held = pltpu.VMEM((NSUB, HALF * ROWS, LANES), F32)
+    send, part, right = pl.pallas_call(
         images,
-        out_shape=(jax.ShapeDtypeStruct(strips, F32), jax.ShapeDtypeStruct(strips, BF)),
+        out_shape=(
+            jax.ShapeDtypeStruct(strips, BF),
+            jax.ShapeDtypeStruct((NSUB, RADIX, J, 2 * F), BF),
+            jax.ShapeDtypeStruct((NSUB * RADIX, 2 * J, 2 * Q), BF),
+        ),
         in_specs=[anywhere] * 6,
-        out_specs=(vmem, vmem),
+        out_specs=(vmem, vmem, vmem),
         scratch_shapes=[
             pltpu.SMEM(shifts.shape, jnp.int32),
             pltpu.SMEM(cover.shape, jnp.int32),
@@ -228,24 +248,39 @@
             pltpu.VMEM((2, F // 2, F), BF),
             pltpu.VMEM((RADIX, 2 * Q, F), BF),
             pltpu.VMEM((RADIX, NSUB * 2 * J, 2 * Q), BF),
-            pltpu.VMEM((NSUB * RADIX, 2 * J, 2 * Q), BF),
-            pltpu.VMEM((NSUB, RADIX, J, 2 * F), BF),
-            pltpu.VMEM((NSUB, SG // RADIX * ROWS, LANES), F32),
+            held,
             pltpu.VMEM((F // 2, LANES), F32),
-            pltpu.SemaphoreType.DMA((7,)),
+            pltpu.SemaphoreType.DMA((5 + 4 * CHUNKS,)),
         ],
-        compiler_params=pltpu.CompilerParams(vmem_limit_bytes=40 * 2**20),
+        compiler_params=pltpu.CompilerParams(vmem_limit_bytes=32 * 2**20),
         name="images",
     )(*given)
     with jax.named_scope("row_swap"):
         other = lax.ppermute(send, "row", [(0, 1), (1, 0)])
+    work = 2 * STRIPS * ROWS * LANES * 2 * Q
+    keep = pl.pallas_call(
+        kept,
+        out_shape=jax.ShapeDtypeStruct(strips, F32),
+        in_specs=[anywhere, anywhere, vmem, vmem],
+        out_specs=vmem,
+        scratch_shapes=[
+            pltpu.SMEM(shifts.shape, jnp.int32),
+            pltpu.SMEM(owner.shape, jnp.int32),
+            held,
+            pltpu.SemaphoreType.DMA((2,)),
+        ],
+        compiler_params=pltpu.CompilerParams(vmem_limit_bytes=16 * 2**20),
+        cost_estimate=pl.CostEstimate(flops=work, bytes_accessed=6 * 2**20, transcendentals=0),
+        name="kept",
+    )(given[0], given[3], *(pltpu.with_memory_space_constraint(x, pltpu.VMEM) for x in (right, part)))
+    with jax.named_scope("row_swap"):
         merged = (keep + other.astype(F32)).astype(BF)
     with jax.named_scope("to_columns"):
         parts = lax.all_to_all(merged, "plane", split_axis=0, concat_axis=0, tiled=True)
     depth = lax.axis_size("line")
     summed = pl.pallas_call(
         column,
-        out_shape=jax.ShapeDtypeStruct((depth, ROWS, LANES), BF),
+        out_shape=pltpu.VMEM((depth, ROWS, LANES), BF),
         in_specs=[vmem],
         out_specs=vmem,
         name="column",

time: 45 us -> 43.5 us (0.967)
  waiting for transfers between devices: 1.9 us -> 0.29 us
    ppermute x1, waiting for transfers between devices: 1.9 us -> 0.29 us  [per_device(): other = lax.ppermute(send, 'row', [(0, 1), (1, 0)])]
    pallas_call x2 -> x3, Pallas kernels: 7.66 us -> 7.81 us  [the longest x1 6.14 us: per_device(): pl.pallas_call(images, out_shape=(jax.ShapeDtypeStruct(strips, BF), jax.S...]
  transfers between devices with their start and end apart: 1 -> 1, of which waited for: 1 -> 1; matrix products, arithmetic and copies ran while one was open for 0% -> 0% of each run, Pallas kernels for 0% -> 4%
where the time goes in v4:
time: 43.5 us; the launch traced here: 43.3 us
  blocking collectives  34.1 us (78%)
  Pallas kernels  8.65 us (20%)
    all_to_all x1, blocking collectives, per_device(): lax.all_to_all(merged, 'plane', split_axis=0, concat_axis=0, tiled=True)  17.8 us
    all_to_all x1, blocking collectives, per_device(): lax.all_to_all(summed, 'line', split_axis=0, concat_axis=0, tiled=True)  16.3 us
    pallas_call x1, Pallas kernels, per_device(): pl.pallas_call(images, out_shape=(jax.ShapeDtypeStruct(strips, BF), jax.S...  6.14 us
    pallas_call x1, Pallas kernels, per_device(): pl.pallas_call(kept, out_shape=jax.ShapeDtypeStruct(strips, F32), in_spec...  1.6 us
  transfers between devices with their start and end apart: 1, of which 1 were waited for; matrix products, arithmetic and copies ran while one was open for 0% of the time, Pallas kernels for 4%

profile of v4, /device:TPU:2, one launch (start us, length us, event | category | flops | bytes accessed | tf_op | source)
XLA Modules:
  0.0 43.3 jit_solution(8193358659239773869)
XLA Ops:
  0.0 6.1 %images.1 = (bf16[128,16,128]{2,1,0:T(8,128)(2,1)S(1)}, bf16[4,4,64,2048]{3,2,1,0:T(8,128)(2,1)S(1)}, bf16[16,128,512]{2,1,0:T(8,128)(2,1)S(1)}) custom-call(s32[1,2,4]{2,1,0:T(2,128)} %shifts_in.3, s32[1,4]{1,0:T(1,128)} %cover_in.1, s32[1,4]{1,0:T(1,128)} %phase_in.1, s32[128]{0:T(128)} %owner_in.3, f32[8,128]{1,0:T(8,128)} %bitcast.1, ...), custom_call_target="tpu_custom_call" | custom-call | tf_op jit(solution)/shard_map/images/pallas_call | solution.py:233
  6.1 0.1 collective-permute-start
  6.2 1.6 %kept.1 = f32[128,16,128]{2,1,0:T(8,128)S(1)} custom-call(s32[1,2,4]{2,1,0:T(2,128)} %shifts_in.3, s32[128]{0:T(128)} %owner_in.3, bf16[16,128,512]{2,1,0:T(8,128)(2,1)S(1)} %get-tuple-element.8.right, bf16[4,4,64,2048]{3,2,1,0:T(8,128)(2,1)S(1)} %get-tuple-element.9.part), custom_call_target="tpu_custom_call" | custom-call | flops 268435456 | bytes 6291456 | tf_op jit(solution)/shard_map/kept/pallas_call | solution.py:261
  7.9 0.3 collective-permute-done
  8.1 0.1 add_convert_fusion
  8.3 17.8 %all_to_all.10.parts = bf16[128,16,128]{2,1,0:T(8,128)(2,1)S(1)} all-to-all(bf16[128,16,128]{2,1,0:T(8,128)(2,1)S(1)} %add_convert_fusion), channel_id=1, replica_groups=mesh['plane'=16,'line'=8,'row'=2] {'plane'}, dimensions={0} | all-to-all | bytes 1048576 | tf_op jit(solution)/shard_map/to_columns/all_to_all | solution.py:279
  26.1 0.1 column.1
  26.2 16.3 %all_to_all.11.parts = bf16[8,16,128]{2,1,0:T(8,128)(2,1)S(1)} all-to-all(bf16[8,16,128]{2,1,0:T(8,128)(2,1)S(1)} %column.1), channel_id=1, replica_groups=mesh['plane'=16,'line'=8,'row'=2] {'line'}, dimensions={0} | all-to-all | bytes 65536 | tf_op jit(solution)/shard_map/to_owners/all_to_all | solution.py:289
  42.4 0.8 %total.1 = f32[1,4,512]{2,1,0:T(4,128)} custom-call(bf16[8,16,128]{2,1,0:T(8,128)(2,1)S(1)} %all_to_all.11.parts), custom_call_target="tpu_custom_call" | custom-call | tf_op jit(solution)/shard_map/total/pallas_call | solution.py:290
Async XLA Ops:
  6.1 2.0 %collective-permute-start = (bf16[128,16,128]{2,1,0:T(8,128)(2,1)S(1)}, bf16[128,16,128]{2,1,0:T(8,128)(2,1)S(1)}, u32[]{:S(2)}, u32[]{:S(2)}) collective-permute-start(bf16[128,16,128]{2,1,0:T(8,128)(2,1)S(1)} %get-tuple-element.10), channel_id=1, source_target_pairs={{0,1},{1,0},{2,3},{3,2},{4,5},{5,4},{6,7},{7,6},{8,9},{9,8},{10,11... | collective-permute-start | bytes 1572872 | tf_op jit(solution)/shard_map/row_swap/ppermute | solution.py:259

commit v5 on v4

--- a/solution.py
+++ b/solution.py
@@ -18,7 +18,6 @@
 ROWS = 16
 LANES = 128
 STEP = 2.0 * math.pi / F
-CHUNKS = 4
 BF = jnp.bfloat16
 F32 = jnp.float32
 
@@ -59,13 +58,9 @@
            shifts, cover, phase, owner, taper, facet, grid, left, strips, columns, sem):
     moves = [(shifts_in, shifts), (cover_in, cover), (phase_in, phase), (owner_in, owner), (taper_in, taper)]
     small = [pltpu.make_async_copy(src, dst, sem.at[n]) for n, (src, dst) in enumerate(moves)]
-    copies = []
-    for g in range(CHUNKS):
-        for p in range(2):
-            for a in range(2):
-                rows = pl.ds(a * Q + g * Q // CHUNKS, Q // CHUNKS)
-                n = len(moves) + len(copies)
-                copies.append(pltpu.make_async_copy(facet_in.at[0, p, rows], facet.at[p, rows], sem.at[n]))
+    copies = [
+        pltpu.make_async_copy(facet_in.at[0, p], facet.at[p], sem.at[len(moves) + p]) for p in range(2)
+    ]
     for copy in small + copies:
         copy.start()
     h = lax.axis_index("row")
@@ -153,29 +148,16 @@
 
     blocks = Q // ROWS
     edges = rim(0)
-
-    def step(i, carry):
-        butterfly(pl.multiple_of(i * ROWS, ROWS), 0, edges)
-        return carry
-
-    for g in range(CHUNKS):
-        for copy in copies[4 * g:4 * g + 4]:
-            copy.wait()
-        lax.fori_loop(g * blocks // CHUNKS, (g + 1) * blocks // CHUNKS, step, 0, unroll=4)
+    for copy in copies:
+        copy.wait()
+    for i in range(blocks):
+        butterfly(i * ROWS, 0, edges)
     tiles = [(c, y) for c in range(RADIX) for y in (0, 2)]
     edges = rim(1)
-    if True:
-        for n, (c, y) in enumerate(tiles):
-            for i in range(n * blocks // 8, (n + 1) * blocks // 8):
-                butterfly(i * ROWS, 1, edges)
-            first(c, 0, y)
-    else:
-        def step1(i, carry):
-            butterfly(pl.multiple_of(i * ROWS, ROWS), 1, edges)
-            return carry
-        lax.fori_loop(0, blocks, step1, 0, unroll=4)
-        for c, y in tiles:
-            first(c, 0, y)
+    for n, (c, y) in enumerate(tiles):
+        for i in range(n * blocks // len(tiles), (n + 1) * blocks // len(tiles)):
+            butterfly(i * ROWS, 1, edges)
+        first(c, 0, y)
     for c, y in tiles:
         first(c, 1, y)
 
@@ -250,7 +232,7 @@
             pltpu.VMEM((RADIX, NSUB * 2 * J, 2 * Q), BF),
             held,
             pltpu.VMEM((F // 2, LANES), F32),
-            pltpu.SemaphoreType.DMA((5 + 4 * CHUNKS,)),
+            pltpu.SemaphoreType.DMA((7,)),
         ],
         compiler_params=pltpu.CompilerParams(vmem_limit_bytes=32 * 2**20),
         name="images",

time: 43.5 us -> 43.1 us (level)
  no operation moved by 1% of the time
where the time goes in v5:
time: 43.1 us; the launch traced here: 42.9 us
  blocking collectives  34.1 us (79%)
  Pallas kernels  8.31 us (19%)
    all_to_all x1, blocking collectives, per_device(): lax.all_to_all(merged, 'plane', split_axis=0, concat_axis=0, tiled=True)  17.8 us
    all_to_all x1, blocking collectives, per_device(): lax.all_to_all(summed, 'line', split_axis=0, concat_axis=0, tiled=True)  16.3 us
    pallas_call x1, Pallas kernels, per_device(): pl.pallas_call(images, out_shape=(jax.ShapeDtypeStruct(strips, BF), jax.S...  5.8 us
    pallas_call x1, Pallas kernels, per_device(): pl.pallas_call(kept, out_shape=jax.ShapeDtypeStruct(strips, F32), in_spec...  1.6 us
  transfers between devices with their start and end apart: 1, of which 1 were waited for; matrix products, arithmetic and copies ran while one was open for 0% of the time, Pallas kernels for 4%

profile of v5, /device:TPU:2, one launch (start us, length us, event | category | flops | bytes accessed | tf_op | source)
XLA Modules:
  0.0 42.9 jit_solution(1305324587300373169)
XLA Ops:
  0.0 5.8 %images.1 = (bf16[128,16,128]{2,1,0:T(8,128)(2,1)S(1)}, bf16[4,4,64,2048]{3,2,1,0:T(8,128)(2,1)S(1)}, bf16[16,128,512]{2,1,0:T(8,128)(2,1)S(1)}) custom-call(s32[1,2,4]{2,1,0:T(2,128)} %shifts_in.3, s32[1,4]{1,0:T(1,128)} %cover_in.1, s32[1,4]{1,0:T(1,128)} %phase_in.1, s32[128]{0:T(128)} %owner_in.3, f32[8,128]{1,0:T(8,128)} %bitcast.1, ...), custom_call_target="tpu_custom_call" | custom-call | tf_op jit(solution)/shard_map/images/pallas_call | solution.py:215
  5.8 0.1 collective-permute-start
  5.9 1.6 %kept.1 = f32[128,16,128]{2,1,0:T(8,128)S(1)} custom-call(s32[1,2,4]{2,1,0:T(2,128)} %shifts_in.3, s32[128]{0:T(128)} %owner_in.3, bf16[16,128,512]{2,1,0:T(8,128)(2,1)S(1)} %get-tuple-element.8.right, bf16[4,4,64,2048]{3,2,1,0:T(8,128)(2,1)S(1)} %get-tuple-element.9.part), custom_call_target="tpu_custom_call" | custom-call | flops 268435456 | bytes 6291456 | tf_op jit(solution)/shard_map/kept/pallas_call | solution.py:243
  7.5 0.3 collective-permute-done
  7.8 0.1 add_convert_fusion
  7.9 17.8 %all_to_all.10.parts = bf16[128,16,128]{2,1,0:T(8,128)(2,1)S(1)} all-to-all(bf16[128,16,128]{2,1,0:T(8,128)(2,1)S(1)} %add_convert_fusion), channel_id=1, replica_groups=mesh['plane'=16,'line'=8,'row'=2] {'plane'}, dimensions={0} | all-to-all | bytes 1048576 | tf_op jit(solution)/shard_map/to_columns/all_to_all | solution.py:261
  25.7 0.1 column.1
  25.8 16.3 %all_to_all.11.parts = bf16[8,16,128]{2,1,0:T(8,128)(2,1)S(1)} all-to-all(bf16[8,16,128]{2,1,0:T(8,128)(2,1)S(1)} %column.1), channel_id=1, replica_groups=mesh['plane'=16,'line'=8,'row'=2] {'line'}, dimensions={0} | all-to-all | bytes 65536 | tf_op jit(solution)/shard_map/to_owners/all_to_all | solution.py:271
  42.1 0.8 %total.1 = f32[1,4,512]{2,1,0:T(4,128)} custom-call(bf16[8,16,128]{2,1,0:T(8,128)(2,1)S(1)} %all_to_all.11.parts), custom_call_target="tpu_custom_call" | custom-call | tf_op jit(solution)/shard_map/total/pallas_call | solution.py:272
Async XLA Ops:
  5.8 2.0 %collective-permute-start = (bf16[128,16,128]{2,1,0:T(8,128)(2,1)S(1)}, bf16[128,16,128]{2,1,0:T(8,128)(2,1)S(1)}, u32[]{:S(2)}, u32[]{:S(2)}) collective-permute-start(bf16[128,16,128]{2,1,0:T(8,128)(2,1)S(1)} %get-tuple-element.10), channel_id=1, source_target_pairs={{0,1},{1,0},{2,3},{3,2},{4,5},{5,4},{6,7},{7,6},{8,9},{9,8},{10,11... | collective-permute-start | bytes 1572872 | tf_op jit(solution)/shard_map/row_swap/ppermute | solution.py:241

commit v6 on v5

--- a/solution.py
+++ b/solution.py
@@ -211,7 +211,7 @@
         pltpu.with_memory_space_constraint(x, pltpu.HBM)
         for x in (shifts, cover, phase, owner, taper.reshape(8, LANES), facet)
     ]
-    held = pltpu.VMEM((NSUB, HALF * ROWS, LANES), F32)
+    held = pltpu.VMEM((NSUB, (HALF + 1) * ROWS, LANES), F32)
     send, part, right = pl.pallas_call(
         images,
         out_shape=(

time: 43.1 us -> 43.1 us (level)
  no operation moved by 1% of the time
where the time goes in v6:
time: 43.1 us; the launch traced here: 42.9 us
  blocking collectives  34.1 us (79%)
  Pallas kernels  8.31 us (19%)
    all_to_all x1, blocking collectives, per_device(): lax.all_to_all(merged, 'plane', split_axis=0, concat_axis=0, tiled=True)  17.8 us
    all_to_all x1, blocking collectives, per_device(): lax.all_to_all(summed, 'line', split_axis=0, concat_axis=0, tiled=True)  16.3 us
    pallas_call x1, Pallas kernels, per_device(): pl.pallas_call(images, out_shape=(jax.ShapeDtypeStruct(strips, BF), jax.S...  5.8 us
    pallas_call x1, Pallas kernels, per_device(): pl.pallas_call(kept, out_shape=jax.ShapeDtypeStruct(strips, F32), in_spec...  1.6 us
  transfers between devices with their start and end apart: 1, of which 1 were waited for; matrix products, arithmetic and copies ran while one was open for 0% of the time, Pallas kernels for 4%

profile of v6, /device:TPU:2, one launch (start us, length us, event | category | flops | bytes accessed | tf_op | source)
XLA Modules:
  0.0 42.9 jit_solution(11604077583026304217)
XLA Ops:
  0.0 5.8 %images.1 = (bf16[128,16,128]{2,1,0:T(8,128)(2,1)S(1)}, bf16[4,4,64,2048]{3,2,1,0:T(8,128)(2,1)S(1)}, bf16[16,128,512]{2,1,0:T(8,128)(2,1)S(1)}) custom-call(s32[1,2,4]{2,1,0:T(2,128)} %shifts_in.3, s32[1,4]{1,0:T(1,128)} %cover_in.1, s32[1,4]{1,0:T(1,128)} %phase_in.1, s32[128]{0:T(128)} %owner_in.3, f32[8,128]{1,0:T(8,128)} %bitcast.1, ...), custom_call_target="tpu_custom_call" | custom-call | tf_op jit(solution)/shard_map/images/pallas_call | solution.py:215
  5.8 0.1 collective-permute-start
  5.9 1.6 %kept.1 = f32[128,16,128]{2,1,0:T(8,128)S(1)} custom-call(s32[1,2,4]{2,1,0:T(2,128)} %shifts_in.3, s32[128]{0:T(128)} %owner_in.3, bf16[16,128,512]{2,1,0:T(8,128)(2,1)S(1)} %get-tuple-element.8.right, bf16[4,4,64,2048]{3,2,1,0:T(8,128)(2,1)S(1)} %get-tuple-element.9.part), custom_call_target="tpu_custom_call" | custom-call | flops 268435456 | bytes 6291456 | tf_op jit(solution)/shard_map/kept/pallas_call | solution.py:243
  7.5 0.3 collective-permute-done
  7.8 0.1 add_convert_fusion
  7.9 17.8 %all_to_all.10.parts = bf16[128,16,128]{2,1,0:T(8,128)(2,1)S(1)} all-to-all(bf16[128,16,128]{2,1,0:T(8,128)(2,1)S(1)} %add_convert_fusion), channel_id=1, replica_groups=mesh['plane'=16,'line'=8,'row'=2] {'plane'}, dimensions={0} | all-to-all | bytes 1048576 | tf_op jit(solution)/shard_map/to_columns/all_to_all | solution.py:261
  25.7 0.1 column.1
  25.8 16.3 %all_to_all.11.parts = bf16[8,16,128]{2,1,0:T(8,128)(2,1)S(1)} all-to-all(bf16[8,16,128]{2,1,0:T(8,128)(2,1)S(1)} %column.1), channel_id=1, replica_groups=mesh['plane'=16,'line'=8,'row'=2] {'line'}, dimensions={0} | all-to-all | bytes 65536 | tf_op jit(solution)/shard_map/to_owners/all_to_all | solution.py:271
  42.1 0.8 %total.1 = f32[1,4,512]{2,1,0:T(4,128)} custom-call(bf16[8,16,128]{2,1,0:T(8,128)(2,1)S(1)} %all_to_all.11.parts), custom_call_target="tpu_custom_call" | custom-call | tf_op jit(solution)/shard_map/total/pallas_call | solution.py:272
Async XLA Ops:
  5.8 2.0 %collective-permute-start = (bf16[128,16,128]{2,1,0:T(8,128)(2,1)S(1)}, bf16[128,16,128]{2,1,0:T(8,128)(2,1)S(1)}, u32[]{:S(2)}, u32[]{:S(2)}) collective-permute-start(bf16[128,16,128]{2,1,0:T(8,128)(2,1)S(1)} %get-tuple-element.10), channel_id=1, source_target_pairs={{0,1},{1,0},{2,3},{3,2},{4,5},{5,4},{6,7},{7,6},{8,9},{9,8},{10,11... | collective-permute-start | bytes 1572872 | tf_op jit(solution)/shard_map/row_swap/ppermute | solution.py:241
